TPU v7x, 768 devices: a whole 4x8x12 slice. The times are simulated.
768 devices in a mesh: section: 6 (over z_hi, core), expert: 4 (over x), dp: 32 (over z_lo, y).
Axes of the slice: x: 4, y: 8, z: 12 (z_hi: 3, z_lo: 4; z = z_hi * 4 + z_lo), core: 2. Of those that a mesh axis runs over, the one named last changes fastest.
Arguments:
- grad_out: bfloat16 [6, 512, 4096], P('section', 'expert', 'dp'), may hold values from -6 to 6
- routes: int32 [6, 512, 2], P('section', 'expert'), may hold values from 0 to 3, all different within a row; in each aligned block of 128 rows (0 to 127, 128 to 255, ..., all dimensions but the last counted through in order) at most 128 rows name the same one
- route_prob: float32 [6, 512, 2], P('section', 'expert'), may hold values from 0.05 to 1
- saved_gate: bfloat16 [6, 4, 512, 768], P('section', 'expert'), may hold values from -6 to 6
- saved_up: bfloat16 [6, 4, 512, 768], P('section', 'expert'), may hold values from -6 to 6
- w_gate: bfloat16 [6, 4, 4096, 768], P('section', 'expert', 'dp'), may hold values from -0.09375 to 0.09375
- w_up: bfloat16 [6, 4, 4096, 768], P('section', 'expert', 'dp'), may hold values from -0.09375 to 0.09375
- w_down: bfloat16 [6, 4, 768, 4096], P('section', 'expert', None, 'dp'), may hold values from -0.21875 to 0.21875
Outputs:
- upstream: bfloat16 [6, 512, 4096], P('section', 'expert', 'dp')
- grad_down: bfloat16 [6, 4, 768, 4096], P('section', 'expert', None, 'dp')
Inputs may be any that keep to these rules, and one draw needn't show every extreme that they name: Each token's 2 ids are distinct; within each aligned block of 128 tokens no expert is named by more than 128 routes, and in every draw some expert is named by exactly 128 routes of some block.
All inputs are finite; a program needn't handle non-finite values.
Results may differ from a plain program's by a relative error of at most 0.0057.
Values may be sent and summed in bfloat16 or wider, within the bound.
A program may use at most 32 MiB of HBM per device.

v0:
```python
import jax
import jax.numpy as jnp
from jax import lax
from jax.sharding import PartitionSpec as P


def from_behind(value, axis, steps):
    count = lax.axis_size(axis)
    first, last = (max(0, -steps), min(count, count - steps))
    return lax.ppermute(value, axis, [(source, source + steps) for source in range(first, last)])


def contract_last(left, right):
    return lax.dot_general(
        left, right, (((1,), (1,)), ((), ())), preferred_element_type=jnp.float32
    )


def contract_first(left, right):
    return lax.dot_general(
        left, right, (((0,), (0,)), ((), ())), preferred_element_type=jnp.float32
    )


def on_device(grad_out, routes, route_prob, saved_gate, saved_up, w_gate, w_up, w_down):
    group_count = lax.axis_size("expert")
    gradient = grad_out[0]
    expert_ids = routes[0]
    token_count, route_count = expert_ids.shape
    features = gradient.shape[1]
    slot_total = saved_gate.shape[2]
    capacity = slot_total // group_count
    flat_ids = expert_ids.reshape(token_count * route_count)
    matches = (flat_ids[:, None] == jnp.arange(group_count, dtype=jnp.int32)[None, :]).astype(
        jnp.int32
    )
    ordinal = jnp.sum((jnp.cumsum(matches, axis=0) - 1) * matches, axis=1)
    slot_index = flat_ids * capacity + ordinal
    placing = (slot_index[:, None] == jnp.arange(slot_total, dtype=jnp.int32)[None, :]).astype(
        jnp.bfloat16
    )
    routed = (route_prob[0][:, :, None] * gradient[:, None, :].astype(jnp.float32)).astype(
        jnp.bfloat16
    )
    routed = routed.reshape(token_count * route_count, features)
    sending = (
        contract_first(placing, routed)
        .astype(jnp.bfloat16)
        .reshape(group_count, capacity, features)
    )
    received = lax.all_to_all(sending, "expert", split_axis=0, concat_axis=0, tiled=True).reshape(
        slot_total, features
    )
    gate_in = saved_gate[0, 0].astype(jnp.float32)
    up_in = saved_up[0, 0].astype(jnp.float32)
    sigmoid_gate = jax.nn.sigmoid(gate_in)
    swished = gate_in * sigmoid_gate
    gate_weight = w_gate[0, 0]
    up_weight = w_up[0, 0]
    partial_grad = contract_last(received, w_down[0, 0])
    act_grad = lax.psum(partial_grad, "dp")
    gate_grad = (act_grad * up_in * sigmoid_gate * (1.0 + gate_in * (1.0 - sigmoid_gate))).astype(
        jnp.bfloat16
    )
    up_grad = (act_grad * swished).astype(jnp.bfloat16)
    slot_grads = contract_last(gate_grad, gate_weight) + contract_last(up_grad, up_weight)
    activated = (swished * up_in).astype(jnp.bfloat16)
    grad_down = contract_first(activated, received).astype(jnp.bfloat16)
    returning = slot_grads.astype(jnp.bfloat16).reshape(group_count, capacity, features)
    returned = lax.all_to_all(returning, "expert", split_axis=0, concat_axis=0, tiled=True).reshape(
        slot_total, features
    )
    picked = jnp.dot(placing, returned, preferred_element_type=jnp.float32)
    picked = picked.reshape(token_count, route_count, features)
    input_grad = (gradient.astype(jnp.float32) + jnp.sum(picked, axis=1)).astype(jnp.bfloat16)
    upstream = from_behind(input_grad, "section", -1)
    return (upstream[None], grad_down[None, None])


def solution(mesh):
    return jax.shard_map(
        on_device,
        mesh=mesh,
        in_specs=(
            P("section", "expert", "dp"),
            P("section", "expert", None),
            P("section", "expert", None),
            P("section", "expert", None, None),
            P("section", "expert", None, None),
            P("section", "expert", "dp", None),
            P("section", "expert", "dp", None),
            P("section", "expert", None, "dp"),
        ),
        out_specs=(P("section", "expert", "dp"), P("section", "expert", None, "dp")),
        check_vma=False,
    )
```

profile of v0, /device:TPU:1, one launch (start us, length us, event | category | flops | bytes accessed | tf_op | source)
XLA Modules:
  0.0 378.3 jit_solution(5353673436879460697)
XLA Ops:
  7.2 0.0 copy-start
  7.2 0.0 all-reduce.2.cloned.1.call-start
  7.2 0.8 copy.12
  8.0 0.1 eq.60
  8.2 0.1 eq.64
  8.3 1.2 reduce-window.6
  9.6 0.1 slice.8
  9.6 0.1 copy.15
  9.8 0.1 copy.16
  9.9 0.1 add_bitcast_fusion
  10.0 0.8 copy.18
  10.8 0.1 mul.70
  10.9 0.8 bitcast_convert_fusion
  11.7 0.4 convolution_convert_fusion.1
  12.2 9.5 %all_to_all.10 = bf16[4,128,128]{2,1,0:T(8,128)(2,1)S(1)} all-to-all(bf16[4,128,128]{2,1,0:T(8,128)(2,1)S(1)} %bitcast.93), channel_id=1, replica_groups=mesh['section'=6,'expert'=4,'dp'=32] {'expert'}, dimensions={0} | all-to-all | bytes 262144 | tf_op jit(solution)/shard_map/all_to_all | solution.py:51
  21.6 0.0 copy-done
  21.6 0.0 copy-start.3
  21.7 0.0 copy-start.4
  21.7 0.0 copy-start.5
  21.7 1.5 fusion.30
  23.2 0.0 all-reduce.2.cloned.1.call-update
  23.2 0.1 reduce_sum.21
  23.3 0.0 copy-start.6
  23.4 302.2 %all-reduce.2.cloned.1.call-done = f32[512,768]{1,0:T(8,128)} async-done(((f32[512,768]{1,0:T(8,128)}), f32[512,768]{1,0:T(8,128)}) %all-reduce.2.cloned.1.call-update) | async-done | bytes 1572880 | tf_op jit(solution)/shard_map/psum | solution.py:61
  325.5 0.0 copy-done.3
  325.5 0.0 copy-done.4
  325.5 0.0 copy-done.5
  325.5 0.0 copy-start.2
  325.5 2.3 fusion.22
  327.8 0.0 copy-done.6
  327.8 0.0 copy-done.2
  327.8 0.0 copy-start.1
  327.9 1.3 fusion.18
  329.1 3.3 all-to-all-start.1
  332.5 0.1 copy.17
  332.5 5.1 %all-to-all-done.1 = bf16[4,128,128]{2,1,0:T(8,128)(2,1)S(1)} async-done(((bf16[4,128,128]{2,1,0:T(8,128)(2,1)}), bf16[4,128,128]{2,1,0:T(8,128)(2,1)S(1)}, u32[]{:S(2)}, u32[]{:S(2)}) %all-to-all-start.1) | async-done | bytes 131104 | tf_op jit(solution)/shard_map/all_to_all | solution.py:70
  337.6 0.3 convolution_reduce_fusion
  337.9 0.0 copy-done.1
  337.9 25.9 %collective-permute-start = (bf16[128,128]{1,0:T(8,128)(2,1)S(1)}, bf16[128,128]{1,0:T(8,128)(2,1)S(1)}, u32[]{:S(2)}, u32[]{:S(2)}) collective-permute-start(bf16[128,128]{1,0:T(8,128)(2,1)S(1)} %add_convert_fusion), channel_id=1, source_target_pairs={{128,0},{256,128},{384,256},{512,384},{640,512},{129,1},{257,129},... | collective-permute-start | bytes 98312 | tf_op jit(solution)/shard_map/ppermute | solution.py:10
  363.9 1.5 fusion.17
  365.3 5.5 %collective-permute-done = bf16[128,128]{1,0:T(8,128)(2,1)S(1)} collective-permute-done((bf16[128,128]{1,0:T(8,128)(2,1)S(1)}, bf16[128,128]{1,0:T(8,128)(2,1)S(1)}, u32[]{:S(2)}, u32[]{:S(2)}) %collective-permute-start) | collective-permute-done | bytes 32800 | tf_op jit(solution)/shard_map/ppermute | solution.py:10
  370.9 0.6 copy.23
  (8 shorter events, 0.1 us)
Async XLA Ops:
  7.2 14.5 %copy-start = (bf16[1,1,768,128]{3,2,1,0:T(8,128)(2,1)S(1)}, bf16[1,1,768,128]{3,2,1,0:T(8,128)(2,1)}, u32[]{:S(2)}) copy-start(bf16[1,1,768,128]{3,2,1,0:T(8,128)(2,1)} %param.15) | copy-start | bytes 589828
  7.2 318.3 %all-reduce.2.cloned.1.call-start = ((), (), s32[]{:S(2)}) async-start(), calls=%async_computation.2 | async-start | bytes 3145728 | tf_op jit(solution)/shard_map/psum | solution.py:61
  21.6 303.9 %copy-start.3 = (bf16[1,1,512,768]{3,2,1,0:T(8,128)(2,1)S(1)}, bf16[1,1,512,768]{3,2,1,0:T(8,128)(2,1)}, u32[]{:S(2)}) copy-start(bf16[1,1,512,768]{3,2,1,0:T(8,128)(2,1)} %param.12) | copy-start | bytes 2359300
  21.7 303.9 %copy-start.4 = (bf16[1,1,512,768]{3,2,1,0:T(8,128)(2,1)S(1)}, bf16[1,1,512,768]{3,2,1,0:T(8,128)(2,1)}, u32[]{:S(2)}) copy-start(bf16[1,1,512,768]{3,2,1,0:T(8,128)(2,1)} %param.11) | copy-start | bytes 2359300
  21.7 303.9 %copy-start.5 = (bf16[1,1,128,768]{3,2,1,0:T(8,128)(2,1)S(1)}, bf16[1,1,128,768]{3,2,1,0:T(8,128)(2,1)}, u32[]{:S(2)}) copy-start(bf16[1,1,128,768]{3,2,1,0:T(8,128)(2,1)} %param.13) | copy-start | bytes 589828
  23.3 304.5 %copy-start.6 = (bf16[1,1,128,768]{3,2,1,0:T(8,128)(2,1)S(1)}, bf16[1,1,128,768]{3,2,1,0:T(8,128)(2,1)}, u32[]{:S(2)}) copy-start(bf16[1,1,128,768]{3,2,1,0:T(8,128)(2,1)} %param.14) | copy-start | bytes 589828
  325.5 2.3 copy-start.2
  327.8 10.1 %copy-start.1 = (bf16[1,128,128]{2,1,0:T(8,128)(2,1)S(1)}, bf16[1,128,128]{2,1,0:T(8,128)(2,1)}, u32[]{:S(2)}) copy-start(bf16[1,128,128]{2,1,0:T(8,128)(2,1)} %param.8) | copy-start | bytes 98308
  329.1 8.5 %all-to-all-start.1 = ((bf16[4,128,128]{2,1,0:T(8,128)(2,1)}), bf16[4,128,128]{2,1,0:T(8,128)(2,1)S(1)}, u32[]{:S(2)}, u32[]{:S(2)}) async-start(bf16[4,128,128]{2,1,0:T(8,128)(2,1)} %bitcast.14), calls=%async_computation.1 | async-start | bytes 262144 | tf_op jit(solution)/shard_map/all_to_all | solution.py:70
  337.9 32.9 %collective-permute-start = (bf16[128,128]{1,0:T(8,128)(2,1)S(1)}, bf16[128,128]{1,0:T(8,128)(2,1)S(1)}, u32[]{:S(2)}, u32[]{:S(2)}) collective-permute-start(bf16[128,128]{1,0:T(8,128)(2,1)S(1)} %add_convert_fusion), channel_id=1, source_target_pairs={{128,0},{256,128},{384,256},{512,384},{640,512},{129,1},{257,129},... | collective-permute-start | bytes 98312 | tf_op jit(solution)/shard_map/ppermute | solution.py:10
Sparse Core Ops, SparseCore 0:
  23.3 302.1 all-reduce.1
where the time goes:
time: 379 us; the launch traced here: 378 us
  waiting for transfers between devices  313 us (83%)
  starting transfers between devices  29.3 us (8%)
  between operations  14.2 us (4%)
  blocking collectives  9.47 us (2%)
  matrix products  7.23 us (2%)
    psum x1, waiting for transfers between devices, on_device(): act_grad = lax.psum(partial_grad, 'dp')  302 us
    ppermute x1, starting transfers between devices, from_behind(): lax.ppermute(value, axis, [(source, source + steps) for source in range(f...  25.9 us
    all_to_all x1, blocking collectives, on_device(): lax.all_to_all(sending, 'expert', split_axis=0, concat_axis=0, tiled=True)  9.47 us
  transfers between devices with their start and end apart: 3, of which 3 were waited for; matrix products, arithmetic and copies ran while one was open for 0% of the time, Pallas kernels for 0%

commit v1 on v0

v1 whole, which is shorter than its diff:
```python
import functools

import jax
import jax.numpy as jnp
from jax import lax
from jax.experimental import pallas as pl
from jax.experimental.pallas import tpu as pltpu
from jax.sharding import PartitionSpec as P

MESH = pl.DeviceIdType.MESH
F32 = jnp.float32
BF16 = jnp.bfloat16

NX, NY, NZ, NS = 4, 8, 4, 6
TOK, FEAT, HID = 128, 128, 768
CA = 384
CB = HID - CA
RY, RZ = TOK // NY, TOK // NZ
Y_ORDER = (4, 3, 5, 2, 6, 1, 7)
Z_ORDER = (2, 1, 3)


def spans(start, stop, step):
    return [(at, min(step, stop - at)) for at in range(start, stop, step)]


def dot_nt(left, right):
    return lax.dot_general(left, right, (((1,), (1,)), ((), ())), preferred_element_type=F32)


def dot_tn(left, right):
    return lax.dot_general(left, right, (((0,), (0,)), ((), ())), preferred_element_type=F32)


def kernel(
    grad_h, routes_h, prob_h, sg_h, su_h, wg_h, wu_h, wd_h,
    up_out, gd_out,
    grads, meta, routes, prob, sg, su, wg, wu, wd,
    pa, pb, ra, rb, sa, sb, r2a, r2b, acta, actb,
    fgate, fup, activated, routed, mine, ret, ubuf, vbuf,
    load_sem, x_send, x_recv, m_recv, s1a_send, s1a_recv, s1b_send, s1b_recv,
    s2a_send, s2a_recv, s2b_send, s2b_recv,
    g1a_send, g1a_recv, g1b_send, g1b_recv, g2a_send, g2a_recv, g2b_send, g2b_recv,
    ret_send, ret_recv, sec_send, sec_recv,
):
    s = lax.axis_index("section")
    x = lax.axis_index("expert")
    d = lax.axis_index("dp")
    y = d % NY
    z = d // NY

    def at_y(k):
        return (y + k) % NY

    def at_z(k):
        return (z + k) % NZ

    def dp(zz, yy):
        return {"dp": zz * NY + yy}

    def copy(src, dst, send, recv, device):
        return pltpu.make_async_remote_copy(
            src_ref=src, dst_ref=dst, send_sem=send, recv_sem=recv,
            device_id=device, device_id_type=MESH,
        )

    def await_recv(ref, sem):
        copy(ref, ref, sem, sem, dp(z, y)).wait_recv()

    def await_send(ref, sem):
        copy(ref, ref, sem, sem, dp(z, y)).wait_send()

    loads = {}
    for number, (name, src, dst) in enumerate((
        ("grad", grad_h, grads.at[0]), ("routes", routes_h, routes), ("prob", prob_h, prob),
        ("wd", wd_h, wd), ("sg", sg_h, sg), ("su", su_h, su), ("wg", wg_h, wg), ("wu", wu_h, wu),
    )):
        loads[name] = pltpu.make_async_copy(src, dst, load_sem.at[number])
        loads[name].start()

    barrier = pltpu.get_barrier_semaphore()
    greet = [dp(z, at_y(k)) for k in range(1, NY)] + [dp(at_z(k), y) for k in range(1, NZ)]
    greet += [{"expert": (x + k) % NX} for k in range(1, NX)]
    greet += [{"section": (s + 1) % NS}]
    for device in greet:
        pl.semaphore_signal(barrier, inc=1, device_id=device, device_id_type=MESH)

    for name in ("grad", "routes", "prob"):
        loads[name].wait()
    meta[0, 0:2, :] = prob[...]
    meta[0, 2:4, :] = routes[...].astype(F32)
    meta[0, 4:8, :] = jnp.zeros((4, TOK), F32)

    def make_partial(j):
        for at, size in spans(0, CA, 256):
            pa[j, :, at:at + size] = dot_nt(grads[j], wd[at:at + size, :]).astype(BF16)
        for at, size in spans(0, CB, 256):
            pb[j, :, at:at + size] = dot_nt(grads[j], wd[CA + at:CA + at + size, :]).astype(BF16)

    loads["wd"].wait()
    make_partial(0)

    pl.semaphore_wait(barrier, len(greet))

    for j in (2, 1, 3):
        device = {"expert": (x + NX - j) % NX}
        copy(grads.at[0], grads.at[j], x_send, x_recv.at[j], device).start()
    for j in (2, 1, 3):
        device = {"expert": (x + NX - j) % NX}
        copy(meta.at[0], meta.at[j], x_send, m_recv.at[j], device).start()

    def send_first(j):
        order = [("y", k) for k in Y_ORDER]
        for place, k in zip((0, 3, 6), Z_ORDER):
            order.insert(place, ("z", k))
        for kind, k in order:
            if kind == "y":
                rows = pl.ds(pl.multiple_of(at_y(k) * RY, RY), RY)
                copy(pa.at[j, rows], ra.at[j, k - 1], s1a_send, s1a_recv.at[j], dp(z, at_y(k))).start()
            else:
                rows = pl.ds(pl.multiple_of(at_z(k) * RZ, RZ), RZ)
                copy(pb.at[j, rows], rb.at[j, k - 1], s1b_send, s1b_recv.at[j], dp(at_z(k), y)).start()

    send_first(0)
    for j in (1, 3, 2):
        await_recv(grads.at[j], x_recv.at[j])
        make_partial(j)
        send_first(j)

    lower = (
        lax.broadcasted_iota(jnp.int32, (TOK, TOK), 0) < lax.broadcasted_iota(jnp.int32, (TOK, TOK), 1)
    ).astype(F32).astype(BF16)
    lane = lax.broadcasted_iota(jnp.int32, (TOK, TOK), 1)

    def make_factors(j):
        group = (x + j) % NX
        me = x.astype(F32)
        rows = meta[j]
        first = rows[2:3] == me
        second = rows[3:4] == me
        weight = jnp.where(first, rows[0:1], 0.0) + jnp.where(second, rows[1:2], 0.0)
        named = jnp.where(first, 1.0, 0.0) + jnp.where(second, 1.0, 0.0)
        named8 = jnp.broadcast_to(named, (8, TOK))
        rank = jnp.dot(named8.astype(BF16), lower, preferred_element_type=F32)[0:1]
        rank = jnp.where(named > 0.0, rank, -1.0)
        row = lax.broadcasted_iota(jnp.int32, (8, TOK), 0)
        columns = jnp.where(row == 0, jnp.broadcast_to(rank, (8, TOK)), jnp.broadcast_to(weight, (8, TOK))).T
        placing = jnp.where(columns[:, 0:1].astype(jnp.int32) == lane, 1.0, 0.0).astype(BF16)
        weight = columns[:, 1:2]
        routed[pl.ds(j * TOK, TOK), :] = (weight * grads[j].astype(F32)).astype(BF16)
        slots = pl.ds(pl.multiple_of(group * TOK, TOK), TOK)
        for at, size in spans(0, HID, 256):
            gate = jnp.dot(placing, sg[slots, at:at + size], preferred_element_type=F32)
            up = jnp.dot(placing, su[slots, at:at + size], preferred_element_type=F32)
            sigmoid = jax.nn.sigmoid(gate)
            swished = gate * sigmoid
            fgate[j, :, at:at + size] = weight * (up * sigmoid * (1.0 + gate * (1.0 - sigmoid)))
            fup[j, :, at:at + size] = weight * swished
            activated[pl.ds(j * TOK, TOK), at:at + size] = (swished * up).astype(BF16)

    my_y = pl.ds(pl.multiple_of(y * RY, RY), RY)
    my_z = pl.ds(pl.multiple_of(z * RZ, RZ), RZ)

    def second(j):
        await_recv(ra.at[j], s1a_recv.at[j])
        total = pa[j, my_y, :].astype(F32)
        for k in range(NY - 1):
            total += ra[j, k].astype(F32)
        sa[j] = total.astype(BF16)

        @pl.when(z != j)
        def _():
            copy(sa.at[j], r2a.at[(j - z + NZ) % NZ - 1], s2a_send, s2a_recv, dp(j, y)).start()

        await_recv(rb.at[j], s1b_recv.at[j])
        total = pb[j, my_z, :].astype(F32)
        for k in range(NZ - 1):
            total += rb[j, k].astype(F32)
        sb[j] = total.astype(BF16)
        for half in range(2):
            owner = 2 * j + half

            @pl.when(y != owner)
            def _():
                copy(
                    sb.at[j, pl.ds(half * 16, 16)], r2b.at[(owner - y + NY) % NY - 1],
                    s2b_send, s2b_recv, dp(z, owner),
                ).start()

    loads["sg"].wait()
    loads["su"].wait()

    def factors(j):
        if j:
            await_recv(meta.at[j], m_recv.at[j])
        make_factors(j)

    factors(0)
    factors(1)
    second(0)
    factors(3)
    second(1)
    factors(2)
    second(3)
    second(2)

    def make_down(at, size):
        gd_out[at:at + size, :] = dot_tn(activated[:, at:at + size], routed[...]).astype(BF16)

    make_down(0, 256)

    await_recv(r2a, s2a_recv)
    total = sa[z].astype(F32)
    for k in range(NZ - 1):
        total += r2a[k].astype(F32)
    acta[z, my_y, :] = total.astype(BF16)
    for k in Z_ORDER:
        copy(acta.at[z, my_y], acta.at[z, my_y], g1a_send, g1a_recv.at[k - 1], dp(at_z(k), y)).start()

    owned = y // 2
    inner = pl.ds(pl.multiple_of((y % 2) * 16, 16), 16)
    owned_rows = pl.ds(pl.multiple_of(z * RZ + (y % 2) * 16, 16), 16)
    await_recv(r2b, s2b_recv)
    total = sb[owned, inner, :].astype(F32)
    for k in range(NY - 1):
        total += r2b[k].astype(F32)
    actb[owned, owned_rows, :] = total.astype(BF16)
    for k in Y_ORDER:
        copy(
            actb.at[owned, owned_rows], actb.at[owned, owned_rows],
            g1b_send, g1b_recv.at[k - 1], dp(z, at_y(k)),
        ).start()

    def gather_y(i):
        j = at_z(i)
        for k in Y_ORDER:
            copy(acta.at[j, my_y], acta.at[j, my_y], g2a_send, g2a_recv.at[i], dp(z, at_y(k))).start()

    def gather_z(i):
        for k in Z_ORDER:
            j = at_z(k + i)
            copy(actb.at[j, my_z], actb.at[j, my_z], g2b_send, g2b_recv.at[i], dp(at_z(k), y)).start()

    gather_y(0)
    make_down(256, 256)
    for k in range(1, NY):
        source = at_y(NY - k)
        rows = pl.ds(pl.multiple_of(z * RZ + (source % 2) * 16, 16), 16)
        await_recv(actb.at[source // 2, rows], g1b_recv.at[k - 1])
    gather_z(0)
    for i in range(1, NZ):
        await_recv(acta.at[at_z(i), my_y], g1a_recv.at[NZ - i - 1])
        gather_y(i)
        gather_z(i)
    make_down(512, 256)

    loads["wg"].wait()
    loads["wu"].wait()

    for i in range(NZ):
        j = at_z(i)
        await_recv(ra.at[i], g2a_recv.at[i])
        await_recv(rb.at[i], g2b_recv.at[i])
        total = jnp.zeros((TOK, FEAT), F32)
        pieces = [(acta, at, at, size) for at, size in spans(0, CA, 256)]
        pieces += [(actb, at, CA + at, size) for at, size in spans(0, CB, 256)]
        for act, at, column, size in pieces:
            value = act[j, :, at:at + size].astype(F32)
            gate = (value * fgate[j, :, column:column + size]).astype(BF16)
            up = (value * fup[j, :, column:column + size]).astype(BF16)
            total += dot_nt(gate, wg[:, column:column + size])
            total += dot_nt(up, wu[:, column:column + size])
        mine[j] = total.astype(BF16)

        @pl.when(j != 0)
        def _():
            copy(mine.at[j], ret.at[j - 1], ret_send, ret_recv, {"expert": (x + j) % NX}).start()

    await_recv(ret, ret_recv)
    total = grads[0].astype(F32)
    returned = mine[0].astype(F32)
    for k in range(NX - 1):
        returned += ret[k].astype(F32)
    ubuf[...] = (total + returned).astype(BF16)
    last = copy(ubuf, vbuf, sec_send, sec_recv, {"section": (s + NS - 1) % NS})
    last.start()

    for j in range(1, NX):
        await_send(grads.at[0], x_send)
        await_send(meta.at[0], x_send)
    for j in range(NX):
        await_send(ra.at[j], s1a_send)
        await_send(rb.at[j], s1b_send)
        await_send(ra.at[j], g2a_send)
        await_send(rb.at[j], g2b_send)
    await_send(r2a, s2a_send)
    await_send(r2a, g1a_send)
    await_send(r2b, g1b_send)
    await_send(r2b, s2b_send)
    await_send(ret, ret_send)

    last.wait_recv()
    up_out[...] = jnp.where(s == NS - 1, jnp.zeros_like(vbuf), vbuf[...])
    last.wait_send()


def on_device(grad_out, routes, route_prob, saved_gate, saved_up, w_gate, w_up, w_down):
    vmem = pltpu.VMEM
    dma = pltpu.SemaphoreType.DMA
    upstream, grad_down = pl.pallas_call(
        kernel,
        out_shape=(
            jax.ShapeDtypeStruct((TOK, FEAT), BF16),
            jax.ShapeDtypeStruct((HID, FEAT), BF16),
        ),
        in_specs=[pl.BlockSpec(memory_space=pltpu.HBM)] * 8,
        out_specs=[pl.BlockSpec(memory_space=vmem)] * 2,
        scratch_shapes=[
            vmem((NX, TOK, FEAT), BF16),
            vmem((NX, 8, TOK), F32),
            vmem((2, TOK), jnp.int32),
            vmem((2, TOK), F32),
            vmem((NX * TOK, HID), BF16),
            vmem((NX * TOK, HID), BF16),
            vmem((FEAT, HID), BF16),
            vmem((FEAT, HID), BF16),
            vmem((HID, FEAT), BF16),
            vmem((NX, TOK, CA), BF16),
            vmem((NX, TOK, CB), BF16),
            vmem((NX, NY - 1, RY, CA), BF16),
            vmem((NX, NZ - 1, RZ, CB), BF16),
            vmem((NX, RY, CA), BF16),
            vmem((NX, RZ, CB), BF16),
            vmem((NZ - 1, RY, CA), BF16),
            vmem((NY - 1, 16, CB), BF16),
            vmem((NX, TOK, CA), BF16),
            vmem((NX, TOK, CB), BF16),
            vmem((NX, TOK, HID), F32),
            vmem((NX, TOK, HID), F32),
            vmem((NX * TOK, HID), BF16),
            vmem((NX * TOK, FEAT), BF16),
            vmem((NX, TOK, FEAT), BF16),
            vmem((NX - 1, TOK, FEAT), BF16),
            vmem((TOK, FEAT), BF16),
            vmem((TOK, FEAT), BF16),
            dma((8,)),
            dma, dma((NX,)), dma((NX,)),
            dma, dma((NX,)), dma, dma((NX,)),
            dma, dma, dma, dma,
            dma, dma((NZ - 1,)), dma, dma((NY - 1,)),
            dma, dma((NZ,)), dma, dma((NZ,)),
            dma, dma, dma, dma,
        ],
        compiler_params=pltpu.CompilerParams(
            collective_id=0, has_side_effects=True, vmem_limit_bytes=48 << 20
        ),
    )(
        grad_out[0], routes[0].T, route_prob[0].T, saved_gate[0, 0], saved_up[0, 0],
        w_gate[0, 0], w_up[0, 0], w_down[0, 0],
    )
    return upstream[None], grad_down[None, None]


def solution(mesh):
    return jax.shard_map(
        on_device,
        mesh=mesh,
        in_specs=(
            P("section", "expert", "dp"),
            P("section", "expert", None),
            P("section", "expert", None),
            P("section", "expert", None, None),
            P("section", "expert", None, None),
            P("section", "expert", "dp", None),
            P("section", "expert", "dp", None),
            P("section", "expert", None, "dp"),
        ),
        out_specs=(P("section", "expert", "dp"), P("section", "expert", None, "dp")),
        check_vma=False,
    )
```

time: 379 us -> 65.8 us (0.17)
  waiting for transfers between devices: 313 us -> 0 us
  Pallas kernels: 0 us -> 57 us
  starting transfers between devices: 29.3 us -> 0 us
  between operations: 14.2 us -> 0.66 us
  blocking collectives: 9.47 us -> 0 us
  matrix products: 7.23 us -> 0 us
  local copies, waits for them, and re-layouts: 3.19 us -> 7.77 us
    psum x1 -> x0, waiting for transfers between devices: 302 us -> none  [on_device(): act_grad = lax.psum(partial_grad, 'dp')]
    pallas_call x0 -> x1, Pallas kernels: none -> 57 us  [on_device(): pl.pallas_call(kernel, out_shape=(jax.ShapeDtypeStruct((TOK, FEAT), BF16)...]
    ppermute x1 -> x0, starting transfers between devices: 25.9 us -> none  [from_behind(): lax.ppermute(value, axis, [(source, source + steps) for source in range(f...]
    all_to_all x1 -> x0, blocking collectives: 9.47 us -> none  [on_device(): lax.all_to_all(sending, 'expert', split_axis=0, concat_axis=0, tiled=True)]
    dot_general x6 -> x0, matrix products: 7.23 us -> none  [the longest x3 5.06 us: contract_last(): lax.dot_general(left, right, (((1,), (1,)), ((), ())), preferred_element_...]
    ppermute x1 -> x0, waiting for transfers between devices: 5.54 us -> none  [from_behind(): lax.ppermute(value, axis, [(source, source + steps) for source in range(f...]
    unnamed x17 -> x18, local copies, waits for them, and re-layouts: 2.26 us -> 7.77 us
    all_to_all x1 -> x0, waiting for transfers between devices: 5.11 us -> none  [on_device(): lax.all_to_all(returning, 'expert', split_axis=0, concat_axis=0, tiled=True)]
  transfers between devices with their start and end apart: 3 -> 0, of which waited for: 3 -> 0; matrix products, arithmetic and copies ran while one was open for 0% -> 0% of each run, Pallas kernels for 0% -> 0%
where the time goes in v1:
time: 65.8 us; the launch traced here: 65.4 us
  Pallas kernels  57 us (87%)
  local copies, waits for them, and re-layouts  7.77 us (12%)
  between operations  0.66 us (1%)
    pallas_call x1, Pallas kernels, on_device(): pl.pallas_call(kernel, out_shape=(jax.ShapeDtypeStruct((TOK, FEAT), BF16)...  57 us
    unnamed x18, local copies, waits for them, and re-layouts  7.77 us

profile of v1, /device:TPU:1, one launch (start us, length us, event | category | flops | bytes accessed | tf_op | source)
XLA Modules:
  0.0 65.4 jit_solution(2386532097245250397)
XLA Ops:
  0.6 0.0 copy-start.7
  0.6 0.0 copy-start.6
  0.7 0.7 %copy-done.7 = f32[1,128,2]{1,2,0:T(2,128)S(1)} copy-done((f32[1,128,2]{1,2,0:T(2,128)S(1)}, f32[1,128,2]{1,2,0:T(2,128)}, u32[]{:S(2)}) %copy-start.7) | copy-done | bytes 1048
  1.3 0.0 copy-done.6
  1.3 0.0 copy-start
  1.3 1.1 %copy-done = bf16[1,1,512,768]{3,2,1,0:T(8,128)(2,1)S(1)} copy-done((bf16[1,1,512,768]{3,2,1,0:T(8,128)(2,1)S(1)}, bf16[1,1,512,768]{3,2,1,0:T(8,128)(2,1)}, u32[]{:S(2)}) %copy-start) | copy-done | bytes 786456
  2.5 0.0 copy-start.1
  2.5 1.1 %copy-done.1 = bf16[1,1,512,768]{3,2,1,0:T(8,128)(2,1)S(1)} copy-done((bf16[1,1,512,768]{3,2,1,0:T(8,128)(2,1)S(1)}, bf16[1,1,512,768]{3,2,1,0:T(8,128)(2,1)}, u32[]{:S(2)}) %copy-start.1) | copy-done | bytes 786456
  3.6 0.0 copy-start.2
  3.6 0.9 %copy-done.2 = bf16[1,1,128,768]{3,2,1,0:T(8,128)(2,1)S(1)} copy-done((bf16[1,1,128,768]{3,2,1,0:T(8,128)(2,1)S(1)}, bf16[1,1,128,768]{3,2,1,0:T(8,128)(2,1)}, u32[]{:S(2)}) %copy-start.2) | copy-done | bytes 196632
  4.5 0.0 copy-start.3
  4.5 0.9 %copy-done.3 = bf16[1,1,128,768]{3,2,1,0:T(8,128)(2,1)S(1)} copy-done((bf16[1,1,128,768]{3,2,1,0:T(8,128)(2,1)S(1)}, bf16[1,1,128,768]{3,2,1,0:T(8,128)(2,1)}, u32[]{:S(2)}) %copy-start.3) | copy-done | bytes 196632
  5.5 0.0 copy-start.4
  5.5 0.9 %copy-done.4 = bf16[1,1,768,128]{3,2,1,0:T(8,128)(2,1)S(1)} copy-done((bf16[1,1,768,128]{3,2,1,0:T(8,128)(2,1)S(1)}, bf16[1,1,768,128]{3,2,1,0:T(8,128)(2,1)}, u32[]{:S(2)}) %copy-start.4) | copy-done | bytes 196632
  6.4 0.0 copy-start.5
  6.4 0.8 %copy-done.5 = bf16[1,128,128]{2,1,0:T(8,128)(2,1)S(1)} copy-done((bf16[1,128,128]{2,1,0:T(8,128)(2,1)S(1)}, bf16[1,128,128]{2,1,0:T(8,128)(2,1)}, u32[]{:S(2)}) %copy-start.5) | copy-done | bytes 32792
  7.1 57.0 %shard_map.95 = (bf16[128,128]{1,0:T(8,128)(2,1)S(1)}, bf16[768,128]{1,0:T(8,128)(2,1)S(1)}) custom-call(bf16[128,128]{1,0:T(8,128)(2,1)S(1)} %bitcast.20, s32[2,128]{1,0:T(2,128)S(1)} %bitcast.22, f32[2,128]{1,0:T(2,128)S(1)} %bitcast.23, bf16[512,768]{1,0:T(8,128)(2,1)S(1)} %bitcast.14, bf16[512,768]{1,0:T(8,128)(2,1)S(1)} %bitcast.15, ...), custom_call_target="tpu_custom_call" | custom-call | tf_op jit(solution)/shard_map/pallas_call | solution.py:310
  64.1 0.6 copy.12
  64.7 0.7 %copy.13 = bf16[1,1,768,128]{3,2,1,0:T(8,128)(2,1)} copy(bf16[1,1,768,128]{3,2,1,0:T(8,128)(2,1)S(1)} %bitcast.19) | data formatting | bytes 393216
Async XLA Ops:
  0.6 0.7 %copy-start.7 = (f32[1,128,2]{1,2,0:T(2,128)S(1)}, f32[1,128,2]{1,2,0:T(2,128)}, u32[]{:S(2)}) copy-start(f32[1,128,2]{1,2,0:T(2,128)} %param.10) | copy-start | bytes 3076
  0.6 0.7 %copy-start.6 = (s32[1,128,2]{1,2,0:T(2,128)S(1)}, s32[1,128,2]{1,2,0:T(2,128)}, u32[]{:S(2)}) copy-start(s32[1,128,2]{1,2,0:T(2,128)} %param.9) | copy-start | bytes 3076
  1.3 1.1 %copy-start = (bf16[1,1,512,768]{3,2,1,0:T(8,128)(2,1)S(1)}, bf16[1,1,512,768]{3,2,1,0:T(8,128)(2,1)}, u32[]{:S(2)}) copy-start(bf16[1,1,512,768]{3,2,1,0:T(8,128)(2,1)} %param.11) | copy-start | bytes 2359300
  2.5 1.1 %copy-start.1 = (bf16[1,1,512,768]{3,2,1,0:T(8,128)(2,1)S(1)}, bf16[1,1,512,768]{3,2,1,0:T(8,128)(2,1)}, u32[]{:S(2)}) copy-start(bf16[1,1,512,768]{3,2,1,0:T(8,128)(2,1)} %param.12) | copy-start | bytes 2359300
  3.6 0.9 %copy-start.2 = (bf16[1,1,128,768]{3,2,1,0:T(8,128)(2,1)S(1)}, bf16[1,1,128,768]{3,2,1,0:T(8,128)(2,1)}, u32[]{:S(2)}) copy-start(bf16[1,1,128,768]{3,2,1,0:T(8,128)(2,1)} %param.13) | copy-start | bytes 589828
  4.5 0.9 %copy-start.3 = (bf16[1,1,128,768]{3,2,1,0:T(8,128)(2,1)S(1)}, bf16[1,1,128,768]{3,2,1,0:T(8,128)(2,1)}, u32[]{:S(2)}) copy-start(bf16[1,1,128,768]{3,2,1,0:T(8,128)(2,1)} %param.14) | copy-start | bytes 589828
  5.5 0.9 %copy-start.4 = (bf16[1,1,768,128]{3,2,1,0:T(8,128)(2,1)S(1)}, bf16[1,1,768,128]{3,2,1,0:T(8,128)(2,1)}, u32[]{:S(2)}) copy-start(bf16[1,1,768,128]{3,2,1,0:T(8,128)(2,1)} %param.15) | copy-start | bytes 589828
  6.4 0.8 %copy-start.5 = (bf16[1,128,128]{2,1,0:T(8,128)(2,1)S(1)}, bf16[1,128,128]{2,1,0:T(8,128)(2,1)}, u32[]{:S(2)}) copy-start(bf16[1,128,128]{2,1,0:T(8,128)(2,1)} %param.8) | copy-start | bytes 98308

commit v2 on v1

v2 whole, which is shorter than its diff:
```python
import functools

import jax
import jax.numpy as jnp
from jax import lax
from jax.experimental import pallas as pl
from jax.experimental.pallas import tpu as pltpu
from jax.sharding import PartitionSpec as P

MESH = pl.DeviceIdType.MESH
F32 = jnp.float32
BF16 = jnp.bfloat16

NX, NY, NZ, NS = 4, 8, 4, 6
TOK, FEAT, HID = 128, 128, 768
CA = HID // 2
RY = TOK // NY
Y_ORDER = (4, 3, 5, 2, 6, 1, 7)


def spans(start, stop, step):
    return [(at, min(step, stop - at)) for at in range(start, stop, step)]


def dot_nt(left, right):
    return lax.dot_general(left, right, (((1,), (1,)), ((), ())), preferred_element_type=F32)


def dot_tn(left, right):
    return lax.dot_general(left, right, (((0,), (0,)), ((), ())), preferred_element_type=F32)


def kernel(
    grad_h, routes_h, prob_h, sg_h, su_h, wg_h, wu_h, wd_h,
    up_out, gd_out,
    grads, other, meta, routes, prob, sg, su, wg, wu, wd, wd_half, wg_half, wu_half,
    pa, ra, sa, r2a, acta,
    fgate, fup, activated, routed, mine, ret, ubuf, vbuf,
    load_sem, x_send, x_recv, m_recv, w_send, w_recv, s1a_send, s1a_recv,
    s2a_send, s2a_recv, g2a_send, g2a_recv,
    ret_send, ret_recv, sec_send, sec_recv,
):
    s = lax.axis_index("section")
    x = lax.axis_index("expert")
    d = lax.axis_index("dp")
    y = d % NY
    z = d // NY

    def at_y(k):
        return (y + k) % NY

    half = z % 2
    twin = z + 1 - 2 * half
    far = (z + 2) % NZ
    my_half = pl.ds(pl.multiple_of(half * CA, CA), CA)
    twin_half = pl.ds(pl.multiple_of((1 - half) * CA, CA), CA)

    def dp(zz, yy):
        return {"dp": zz * NY + yy}

    def copy(src, dst, send, recv, device):
        return pltpu.make_async_remote_copy(
            src_ref=src, dst_ref=dst, send_sem=send, recv_sem=recv,
            device_id=device, device_id_type=MESH,
        )

    def await_recv(ref, sem):
        copy(ref, ref, sem, sem, dp(z, y)).wait_recv()

    def await_send(ref, sem):
        copy(ref, ref, sem, sem, dp(z, y)).wait_send()

    sent = []

    loads = {}
    for number, (name, src, dst) in enumerate((
        ("grad", grad_h, grads.at[0]), ("routes", routes_h, routes), ("prob", prob_h, prob),
        ("wd", wd_h, wd), ("sg", sg_h, sg), ("su", su_h, su), ("wg", wg_h, wg), ("wu", wu_h, wu),
    )):
        loads[name] = pltpu.make_async_copy(src, dst, load_sem.at[number])
        loads[name].start()

    barrier = pltpu.get_barrier_semaphore()
    greet = [dp(z, at_y(k)) for k in range(1, NY)] + [dp(far, y)]
    greet += [{"expert": (x + k) % NX} for k in range(1, NX)]
    greet += [{"expert": (x + k) % NX, "dp": twin * NY + y} for k in range(NX)]
    greet += [{"section": (s + 1) % NS}]
    for device in greet:
        pl.semaphore_signal(barrier, inc=1, device_id=device, device_id_type=MESH)

    for name in ("grad", "routes", "prob"):
        loads[name].wait()
    meta[0, 0:2, :] = prob[...]
    meta[0, 2:4, :] = routes[...].astype(F32)
    meta[0, 4:8, :] = jnp.zeros((4, TOK), F32)

    def own_partial(j):
        return dot_nt(grads[j], wd[my_half, :])

    def make_partial(j, own):
        pa[j] = (own + dot_nt(other[j], wd_half[...])).astype(BF16)

    loads["wd"].wait()
    own = own_partial(0)

    pl.semaphore_wait(barrier, len(greet))

    def to_twin(src, dst, send, recv, j):
        copy(src, dst, send, recv, {"expert": (x + NX - j) % NX, "dp": twin * NY + y}).start()

    to_twin(grads.at[0], other.at[0], x_send, x_recv.at[1, 0], 0)
    to_twin(wd.at[twin_half], wd_half, w_send, w_recv.at[0], 0)
    for j in (2, 1, 3):
        to_twin(grads.at[0], other.at[j], x_send, x_recv.at[1, j], j)
        device = {"expert": (x + NX - j) % NX}
        copy(grads.at[0], grads.at[j], x_send, x_recv.at[0, j], device).start()
    for j in (2, 1, 3):
        device = {"expert": (x + NX - j) % NX}
        copy(meta.at[0], meta.at[j], x_send, m_recv.at[j], device).start()
    sent.extend([(grads, x_send), (grads.at[pl.ds(0, 3)], x_send)] + [(meta.at[0], x_send)] * 3)

    def tiles(count):
        return pa.at[0, pl.ds(0, 16 * count)]

    def rows_y(k):
        return pl.ds(pl.multiple_of(at_y(k) * RY, RY), RY)

    def to_y(src, dst, send, recv, k):
        copy(src, dst, send, recv, dp(z, at_y(k))).start()

    def send_first(j):
        for k in Y_ORDER:
            to_y(pa.at[j, rows_y(k)], ra.at[j, k - 1], s1a_send, s1a_recv.at[j], k)
        sent.append((tiles(7), s1a_send))

    await_recv(wd_half, w_recv.at[0])
    await_recv(other.at[0], x_recv.at[1, 0])
    make_partial(0, own)
    send_first(0)
    for j in (1, 3, 2):
        await_recv(grads.at[j], x_recv.at[0, j])
        own = own_partial(j)
        await_recv(other.at[j], x_recv.at[1, j])
        make_partial(j, own)
        send_first(j)

    loads["wg"].wait()
    loads["wu"].wait()
    to_twin(wg.at[:, twin_half], wg_half, w_send, w_recv.at[1], 0)
    to_twin(wu.at[:, twin_half], wu_half, w_send, w_recv.at[2], 0)
    sent.extend([(wd_half, w_send), (wg_half, w_send), (wu_half, w_send)])

    lower = (
        lax.broadcasted_iota(jnp.int32, (TOK, TOK), 0) < lax.broadcasted_iota(jnp.int32, (TOK, TOK), 1)
    ).astype(F32).astype(BF16)
    lane = lax.broadcasted_iota(jnp.int32, (TOK, TOK), 1)

    def make_factors(j):
        group = (x + j) % NX
        me = x.astype(F32)
        rows = meta[j]
        first = rows[2:3] == me
        second = rows[3:4] == me
        weight = jnp.where(first, rows[0:1], 0.0) + jnp.where(second, rows[1:2], 0.0)
        named = jnp.where(first, 1.0, 0.0) + jnp.where(second, 1.0, 0.0)
        named8 = jnp.broadcast_to(named, (8, TOK))
        rank = jnp.dot(named8.astype(BF16), lower, preferred_element_type=F32)[0:1]
        rank = jnp.where(named > 0.0, rank, -1.0)
        row = lax.broadcasted_iota(jnp.int32, (8, TOK), 0)
        columns = jnp.where(row == 0, jnp.broadcast_to(rank, (8, TOK)), jnp.broadcast_to(weight, (8, TOK))).T
        placing = jnp.where(columns[:, 0:1].astype(jnp.int32) == lane, 1.0, 0.0).astype(BF16)
        weight = columns[:, 1:2]
        routed[pl.ds(j * TOK, TOK), :] = (weight * grads[j].astype(F32)).astype(BF16)
        slots = pl.ds(pl.multiple_of(group * TOK, TOK), TOK)
        for side, columns in ((0, my_half), (1, twin_half)):
            gate = jnp.dot(placing, sg[slots, columns], preferred_element_type=F32)
            up = jnp.dot(placing, su[slots, columns], preferred_element_type=F32)
            sigmoid = jax.nn.sigmoid(gate)
            swished = gate * sigmoid
            if side == 0:
                fgate[j] = weight * (up * sigmoid * (1.0 + gate * (1.0 - sigmoid)))
                fup[j] = weight * swished
            activated[pl.ds(j * TOK, TOK), columns] = (swished * up).astype(BF16)

    my_y = pl.ds(pl.multiple_of(y * RY, RY), RY)

    def second(j):
        await_recv(tiles(7), s1a_recv.at[j])
        total = pa[j, my_y, :].astype(F32)
        for k in range(NY - 1):
            total += ra[j, k].astype(F32)
        sa[j] = total.astype(BF16)
        copy(sa.at[j], r2a.at[j], s2a_send, s2a_recv.at[j], dp(far, y)).start()
        sent.append((tiles(1), s2a_send))

    loads["sg"].wait()
    loads["su"].wait()

    def factors(j):
        if j:
            await_recv(meta.at[j], m_recv.at[j])
        make_factors(j)

    factors(0)
    second(0)
    factors(1)
    second(1)
    factors(3)
    second(3)
    factors(2)
    second(2)

    def make_down(at, size):
        gd_out[at:at + size, :] = dot_tn(activated[:, at:at + size], routed[...]).astype(BF16)

    def third(j):
        await_recv(r2a.at[j], s2a_recv.at[j])
        total = sa[j].astype(F32) + r2a[j].astype(F32)
        acta[j, my_y, :] = total.astype(BF16)
        mine_a = acta.at[j, my_y]
        for k in Y_ORDER:
            to_y(mine_a, mine_a, g2a_send, g2a_recv.at[j], k)
        sent.append((tiles(7), g2a_send))

    third(0)
    third(1)
    third(3)
    third(2)
    make_down(0, 256)
    make_down(256, 256)
    make_down(512, 256)

    await_recv(wg_half, w_recv.at[1])
    await_recv(wu_half, w_recv.at[2])

    for j in (1, 3, 2, 0):
        await_recv(tiles(7), g2a_recv.at[j])
        value = acta[j].astype(F32)
        gate = (value * fgate[j]).astype(BF16)
        up = (value * fup[j]).astype(BF16)
        device = {"expert": (x + j) % NX, "dp": twin * NY + y}
        mine[1, j] = (dot_nt(gate, wg_half[...]) + dot_nt(up, wu_half[...])).astype(BF16)
        copy(mine.at[1, j], ret.at[1, j], ret_send, ret_recv.at[1, j], device).start()
        mine[0, j] = (dot_nt(gate, wg[:, my_half]) + dot_nt(up, wu[:, my_half])).astype(BF16)
        if j:
            device = {"expert": (x + j) % NX}
            copy(mine.at[0, j], ret.at[0, j], ret_send, ret_recv.at[0, j], device).start()

    sent.extend([(grads, ret_send), (grads.at[pl.ds(0, 3)], ret_send)])
    for j in (1, 3, 2, 0):
        await_recv(ret.at[1, j], ret_recv.at[1, j])
        if j:
            await_recv(ret.at[0, j], ret_recv.at[0, j])
    total = grads[0].astype(F32)
    returned = mine[0, 0].astype(F32) + ret[1, 0].astype(F32)
    for j in range(1, NX):
        returned += ret[0, j].astype(F32) + ret[1, j].astype(F32)
    ubuf[...] = (total + returned).astype(BF16)
    last = copy(ubuf, vbuf, sec_send, sec_recv, {"section": (s + NS - 1) % NS})
    last.start()

    for ref, sem in sent:
        await_send(ref, sem)
    last.wait_recv()
    up_out[...] = jnp.where(s == NS - 1, jnp.zeros_like(vbuf), vbuf[...])
    last.wait_send()


def on_device(grad_out, routes, route_prob, saved_gate, saved_up, w_gate, w_up, w_down):
    vmem = pltpu.VMEM
    dma = pltpu.SemaphoreType.DMA
    upstream, grad_down = pl.pallas_call(
        kernel,
        out_shape=(
            jax.ShapeDtypeStruct((TOK, FEAT), BF16),
            jax.ShapeDtypeStruct((HID, FEAT), BF16),
        ),
        in_specs=[pl.BlockSpec(memory_space=pltpu.HBM)] * 8,
        out_specs=[pl.BlockSpec(memory_space=vmem)] * 2,
        scratch_shapes=[
            vmem((NX, TOK, FEAT), BF16),
            vmem((NX, TOK, FEAT), BF16),
            vmem((NX, 8, TOK), F32),
            vmem((2, TOK), jnp.int32),
            vmem((2, TOK), F32),
            vmem((NX * TOK, HID), BF16),
            vmem((NX * TOK, HID), BF16),
            vmem((FEAT, HID), BF16),
            vmem((FEAT, HID), BF16),
            vmem((HID, FEAT), BF16),
            vmem((CA, FEAT), BF16),
            vmem((FEAT, CA), BF16),
            vmem((FEAT, CA), BF16),
            vmem((NX, TOK, CA), BF16),
            vmem((NX, NY - 1, RY, CA), BF16),
            vmem((NX, RY, CA), BF16),
            vmem((NX, RY, CA), BF16),
            vmem((NX, TOK, CA), BF16),
            vmem((NX, TOK, CA), F32),
            vmem((NX, TOK, CA), F32),
            vmem((NX * TOK, HID), BF16),
            vmem((NX * TOK, FEAT), BF16),
            vmem((2, NX, TOK, FEAT), BF16),
            vmem((2, NX, TOK, FEAT), BF16),
            vmem((TOK, FEAT), BF16),
            vmem((TOK, FEAT), BF16),
            dma((8,)),
            dma, dma((2, NX)), dma((NX,)),
            dma, dma((3,)), dma, dma((NX,)),
            dma, dma((NX,)), dma, dma((NX,)),
            dma, dma((2, NX)), dma, dma,
        ],
        compiler_params=pltpu.CompilerParams(
            collective_id=0, has_side_effects=True, vmem_limit_bytes=48 << 20
        ),
    )(*(
        pltpu.with_memory_space_constraint(value, pltpu.HBM)
        for value in (
            grad_out[0], routes[0].T, route_prob[0].T, saved_gate[0, 0], saved_up[0, 0],
            w_gate[0, 0], w_up[0, 0], w_down[0, 0],
        )
    ))
    return upstream[None], grad_down[None, None]


def solution(mesh):
    return jax.shard_map(
        on_device,
        mesh=mesh,
        in_specs=(
            P("section", "expert", "dp"),
            P("section", "expert", None),
            P("section", "expert", None),
            P("section", "expert", None, None),
            P("section", "expert", None, None),
            P("section", "expert", "dp", None),
            P("section", "expert", "dp", None),
            P("section", "expert", None, "dp"),
        ),
        out_specs=(P("section", "expert", "dp"), P("section", "expert", None, "dp")),
        check_vma=False,
    )
```

time: 65.8 us -> 53.5 us (0.81)
  local copies, waits for them, and re-layouts: 7.77 us -> 1.29 us
  Pallas kernels: 57 us -> 51.4 us
    unnamed x18 -> x2, local copies, waits for them, and re-layouts: 7.77 us -> 1.29 us
    pallas_call x1, Pallas kernels: 57 us -> 51.4 us  [on_device(): pl.pallas_call(kernel, out_shape=(jax.ShapeDtypeStruct((TOK, FEAT), BF16)...]
where the time goes in v2:
time: 53.5 us; the launch traced here: 53.4 us
  Pallas kernels  51.4 us (96%)
  local copies, waits for them, and re-layouts  1.29 us (2%)
  between operations  0.64 us (1%)
    pallas_call x1, Pallas kernels, on_device(): pl.pallas_call(kernel, out_shape=(jax.ShapeDtypeStruct((TOK, FEAT), BF16)...  51.4 us
    unnamed x2, local copies, waits for them, and re-layouts  1.29 us

profile of v2, /device:TPU:1, one launch (start us, length us, event | category | flops | bytes accessed | tf_op | source)
XLA Modules:
  0.0 53.4 jit_solution(5904984735004270363)
XLA Ops:
  0.6 51.4 %shard_map.95 = (bf16[128,128]{1,0:T(8,128)(2,1)S(1)}, bf16[768,128]{1,0:T(8,128)(2,1)S(1)}) custom-call(bf16[128,128]{1,0:T(8,128)(2,1)} %bitcast.21, s32[2,128]{1,0:T(2,128)} %bitcast.22, f32[2,128]{1,0:T(2,128)} %bitcast.23, bf16[512,768]{1,0:T(8,128)(2,1)} %bitcast.16, bf16[512,768]{1,0:T(8,128)(2,1)} %bitcast.17, bf16[128,768]{1,0:T(8,128)(2,1)} %bitcast.18, ...), custom_call_target="tpu_custom_call" | custom-call | tf_op jit(solution)/shard_map/pallas_call | solution.py:272
  52.1 0.6 %copy.12 = bf16[1,128,128]{2,1,0:T(8,128)(2,1)} copy(bf16[1,128,128]{2,1,0:T(8,128)(2,1)S(1)} %bitcast.15) | data formatting | bytes 65536
  52.7 0.7 %copy.13 = bf16[1,1,768,128]{3,2,1,0:T(8,128)(2,1)} copy(bf16[1,1,768,128]{3,2,1,0:T(8,128)(2,1)S(1)} %bitcast.14) | data formatting | bytes 393216

commit v3 on v2

--- a/solution.py
+++ b/solution.py
@@ -38,7 +38,7 @@
     fgate, fup, activated, routed, mine, ret, ubuf, vbuf,
     load_sem, x_send, x_recv, m_recv, w_send, w_recv, s1a_send, s1a_recv,
     s2a_send, s2a_recv, g2a_send, g2a_recv,
-    ret_send, ret_recv, sec_send, sec_recv,
+    ret_send, ret_recv, sec_send, sec_recv, turn,
 ):
     s = lax.axis_index("section")
     x = lax.axis_index("expert")
@@ -70,8 +70,9 @@
     def await_send(ref, sem):
         copy(ref, ref, sem, sem, dp(z, y)).wait_send()
 
-    sent = []
-
+    live = s != 0
+    first_half = jnp.logical_and(live, s % 2 == 0)
+    second_half = s % 2 == 1
     loads = {}
     for number, (name, src, dst) in enumerate((
         ("grad", grad_h, grads.at[0]), ("routes", routes_h, routes), ("prob", prob_h, prob),
@@ -84,8 +85,20 @@
     greet = [dp(z, at_y(k)) for k in range(1, NY)] + [dp(far, y)]
     greet += [{"expert": (x + k) % NX} for k in range(1, NX)]
     greet += [{"expert": (x + k) % NX, "dp": twin * NY + y} for k in range(NX)]
-    greet += [{"section": (s + 1) % NS}]
     for device in greet:
+        pl.semaphore_signal(barrier, inc=1, device_id=device, device_id_type=MESH)
+    expected = len(greet) + jnp.where(s > 0, 1, 0)
+
+    @pl.when(s < NS - 1)
+    def _():
+        device = {"section": (s + 1) % NS}
+        pl.semaphore_signal(barrier, inc=1, device_id=device, device_id_type=MESH)
+
+    expected += jnp.where(s % 2 == 0, 1, 0)
+
+    @pl.when(s % 2 == 1)
+    def _():
+        device = {"section": (s + NS - 1) % NS}
         pl.semaphore_signal(barrier, inc=1, device_id=device, device_id_type=MESH)
 
     for name in ("grad", "routes", "prob"):
@@ -103,7 +116,14 @@
     loads["wd"].wait()
     own = own_partial(0)
 
-    pl.semaphore_wait(barrier, len(greet))
+    pl.semaphore_wait(barrier, expected)
+
+    def pass_turn():
+        pl.semaphore_signal(turn, inc=1, device_id={"section": (s + 1) % NS}, device_id_type=MESH)
+
+    @pl.when(s == 0)
+    def _():
+        pass_turn()
 
     def to_twin(src, dst, send, recv, j):
         copy(src, dst, send, recv, {"expert": (x + NX - j) % NX, "dp": twin * NY + y}).start()
@@ -117,7 +137,6 @@
     for j in (2, 1, 3):
         device = {"expert": (x + NX - j) % NX}
         copy(meta.at[0], meta.at[j], x_send, m_recv.at[j], device).start()
-    sent.extend([(grads, x_send), (grads.at[pl.ds(0, 3)], x_send)] + [(meta.at[0], x_send)] * 3)
 
     def tiles(count):
         return pa.at[0, pl.ds(0, 16 * count)]
@@ -131,24 +150,6 @@
     def send_first(j):
         for k in Y_ORDER:
             to_y(pa.at[j, rows_y(k)], ra.at[j, k - 1], s1a_send, s1a_recv.at[j], k)
-        sent.append((tiles(7), s1a_send))
-
-    await_recv(wd_half, w_recv.at[0])
-    await_recv(other.at[0], x_recv.at[1, 0])
-    make_partial(0, own)
-    send_first(0)
-    for j in (1, 3, 2):
-        await_recv(grads.at[j], x_recv.at[0, j])
-        own = own_partial(j)
-        await_recv(other.at[j], x_recv.at[1, j])
-        make_partial(j, own)
-        send_first(j)
-
-    loads["wg"].wait()
-    loads["wu"].wait()
-    to_twin(wg.at[:, twin_half], wg_half, w_send, w_recv.at[1], 0)
-    to_twin(wu.at[:, twin_half], wu_half, w_send, w_recv.at[2], 0)
-    sent.extend([(wd_half, w_send), (wg_half, w_send), (wu_half, w_send)])
 
     lower = (
         lax.broadcasted_iota(jnp.int32, (TOK, TOK), 0) < lax.broadcasted_iota(jnp.int32, (TOK, TOK), 1)
@@ -182,6 +183,40 @@
                 fup[j] = weight * swished
             activated[pl.ds(j * TOK, TOK), columns] = (swished * up).astype(BF16)
 
+    def factors(j):
+        if j:
+            await_recv(meta.at[j], m_recv.at[j])
+        make_factors(j)
+
+    await_recv(wd_half, w_recv.at[0])
+    await_recv(other.at[0], x_recv.at[1, 0])
+    make_partial(0, own)
+
+    @pl.when(first_half)
+    def _():
+        send_first(0)
+
+    loads["sg"].wait()
+    loads["su"].wait()
+    factors(0)
+    for j in (1, 3, 2):
+        await_recv(grads.at[j], x_recv.at[0, j])
+        own = own_partial(j)
+        await_recv(other.at[j], x_recv.at[1, j])
+        make_partial(j, own)
+
+        @pl.when(first_half)
+        def _():
+            send_first(j)
+
+    loads["wg"].wait()
+    loads["wu"].wait()
+
+    @pl.when(live)
+    def _():
+        to_twin(wg.at[:, twin_half], wg_half, w_send, w_recv.at[1], 0)
+        to_twin(wu.at[:, twin_half], wu_half, w_send, w_recv.at[2], 0)
+
     my_y = pl.ds(pl.multiple_of(y * RY, RY), RY)
 
     def second(j):
@@ -191,24 +226,10 @@
             total += ra[j, k].astype(F32)
         sa[j] = total.astype(BF16)
         copy(sa.at[j], r2a.at[j], s2a_send, s2a_recv.at[j], dp(far, y)).start()
-        sent.append((tiles(1), s2a_send))
-
-    loads["sg"].wait()
-    loads["su"].wait()
-
-    def factors(j):
-        if j:
-            await_recv(meta.at[j], m_recv.at[j])
-        make_factors(j)
-
-    factors(0)
-    second(0)
+
     factors(1)
-    second(1)
     factors(3)
-    second(3)
     factors(2)
-    second(2)
 
     def make_down(at, size):
         gd_out[at:at + size, :] = dot_tn(activated[:, at:at + size], routed[...]).astype(BF16)
@@ -220,50 +241,92 @@
         mine_a = acta.at[j, my_y]
         for k in Y_ORDER:
             to_y(mine_a, mine_a, g2a_send, g2a_recv.at[j], k)
-        sent.append((tiles(7), g2a_send))
-
-    third(0)
-    third(1)
-    third(3)
-    third(2)
-    make_down(0, 256)
-    make_down(256, 256)
-    make_down(512, 256)
-
-    await_recv(wg_half, w_recv.at[1])
-    await_recv(wu_half, w_recv.at[2])
-
-    for j in (1, 3, 2, 0):
-        await_recv(tiles(7), g2a_recv.at[j])
-        value = acta[j].astype(F32)
-        gate = (value * fgate[j]).astype(BF16)
-        up = (value * fup[j]).astype(BF16)
-        device = {"expert": (x + j) % NX, "dp": twin * NY + y}
-        mine[1, j] = (dot_nt(gate, wg_half[...]) + dot_nt(up, wu_half[...])).astype(BF16)
-        copy(mine.at[1, j], ret.at[1, j], ret_send, ret_recv.at[1, j], device).start()
-        mine[0, j] = (dot_nt(gate, wg[:, my_half]) + dot_nt(up, wu[:, my_half])).astype(BF16)
-        if j:
-            device = {"expert": (x + j) % NX}
-            copy(mine.at[0, j], ret.at[0, j], ret_send, ret_recv.at[0, j], device).start()
-
-    sent.extend([(grads, ret_send), (grads.at[pl.ds(0, 3)], ret_send)])
-    for j in (1, 3, 2, 0):
-        await_recv(ret.at[1, j], ret_recv.at[1, j])
-        if j:
-            await_recv(ret.at[0, j], ret_recv.at[0, j])
-    total = grads[0].astype(F32)
-    returned = mine[0, 0].astype(F32) + ret[1, 0].astype(F32)
+
+    def reduce_rest():
+        second(3)
+        second(2)
+        for j in (1, 3, 2, 0):
+            third(j)
+
+    @pl.when(first_half)
+    def _():
+        second(0)
+        second(1)
+        for j in range(NX):
+            await_send(tiles(7), s1a_send)
+        pass_turn()
+        reduce_rest()
+
+    @pl.when(second_half)
+    def _():
+        pl.semaphore_wait(turn, 1)
+        for j in (0, 1, 3, 2):
+            send_first(j)
+        second(0)
+        second(1)
+        reduce_rest()
+        for j in range(NX):
+            await_send(tiles(7), s1a_send)
+
+
+    last = copy(ubuf, vbuf, sec_send, sec_recv, {"section": (s + NS - 1) % NS})
+
+    @pl.when(live)
+    def _():
+        await_recv(wg_half, w_recv.at[1])
+        await_recv(wu_half, w_recv.at[2])
+        for j in (1, 3, 2, 0):
+            await_recv(tiles(7), g2a_recv.at[j])
+            value = acta[j].astype(F32)
+            gate = (value * fgate[j]).astype(BF16)
+            up = (value * fup[j]).astype(BF16)
+            device = {"expert": (x + j) % NX, "dp": twin * NY + y}
+            mine[1, j] = (dot_nt(gate, wg_half[...]) + dot_nt(up, wu_half[...])).astype(BF16)
+            copy(mine.at[1, j], ret.at[1, j], ret_send, ret_recv.at[1, j], device).start()
+            mine[0, j] = (dot_nt(gate, wg[:, my_half]) + dot_nt(up, wu[:, my_half])).astype(BF16)
+            if j:
+                device = {"expert": (x + j) % NX}
+                copy(mine.at[0, j], ret.at[0, j], ret_send, ret_recv.at[0, j], device).start()
+
+        make_down(0, 256)
+        for j in (1, 3, 2, 0):
+            await_recv(ret.at[1, j], ret_recv.at[1, j])
+            if j:
+                await_recv(ret.at[0, j], ret_recv.at[0, j])
+        total = grads[0].astype(F32)
+        returned = mine[0, 0].astype(F32) + ret[1, 0].astype(F32)
+        for j in range(1, NX):
+            returned += ret[0, j].astype(F32) + ret[1, j].astype(F32)
+        ubuf[...] = (total + returned).astype(BF16)
+        last.start()
+        make_down(256, 256)
+        make_down(512, 256)
+        for ref, sem in (
+            [(wg_half, w_send), (wu_half, w_send), (grads, ret_send), (grads.at[pl.ds(0, 3)], ret_send)]
+            + [(tiles(4), s2a_send)] + [(tiles(7), g2a_send)] * NX
+        ):
+            await_send(ref, sem)
+        last.wait_send()
+
+    @pl.when(s == 0)
+    def _():
+        for at in (0, 256, 512):
+            make_down(at, 256)
+
+    await_send(wd_half, w_send)
+    await_send(grads, x_send)
+    await_send(grads.at[pl.ds(0, 3)], x_send)
     for j in range(1, NX):
-        returned += ret[0, j].astype(F32) + ret[1, j].astype(F32)
-    ubuf[...] = (total + returned).astype(BF16)
-    last = copy(ubuf, vbuf, sec_send, sec_recv, {"section": (s + NS - 1) % NS})
-    last.start()
-
-    for ref, sem in sent:
-        await_send(ref, sem)
-    last.wait_recv()
-    up_out[...] = jnp.where(s == NS - 1, jnp.zeros_like(vbuf), vbuf[...])
-    last.wait_send()
+        await_send(meta.at[0], x_send)
+
+    @pl.when(s == NS - 1)
+    def _():
+        up_out[...] = jnp.zeros_like(up_out)
+
+    @pl.when(s != NS - 1)
+    def _():
+        last.wait_recv()
+        up_out[...] = vbuf[...]
 
 
 def on_device(grad_out, routes, route_prob, saved_gate, saved_up, w_gate, w_up, w_down):
@@ -309,6 +372,7 @@
             dma, dma((3,)), dma, dma((NX,)),
             dma, dma((NX,)), dma, dma((NX,)),
             dma, dma((2, NX)), dma, dma,
+            pltpu.SemaphoreType.REGULAR,
         ],
         compiler_params=pltpu.CompilerParams(
             collective_id=0, has_side_effects=True, vmem_limit_bytes=48 << 20

time: 53.5 us -> 51.7 us (0.966)
  Pallas kernels: 51.4 us -> 49.6 us
    pallas_call x1, Pallas kernels: 51.4 us -> 49.6 us  [on_device(): pl.pallas_call(kernel, out_shape=(jax.ShapeDtypeStruct((TOK, FEAT), BF16)...]
where the time goes in v3:
time: 51.7 us; the launch traced here: 51.5 us
  Pallas kernels  49.6 us (96%)
  local copies, waits for them, and re-layouts  1.29 us (2%)
  between operations  0.64 us (1%)
    pallas_call x1, Pallas kernels, on_device(): pl.pallas_call(kernel, out_shape=(jax.ShapeDtypeStruct((TOK, FEAT), BF16)...  49.6 us
    unnamed x2, local copies, waits for them, and re-layouts  1.29 us

profile of v3, /device:TPU:1, one launch (start us, length us, event | category | flops | bytes accessed | tf_op | source)
XLA Modules:
  0.0 51.5 jit_solution(10960383298838751737)
XLA Ops:
  0.6 49.6 %shard_map.95 = (bf16[128,128]{1,0:T(8,128)(2,1)S(1)}, bf16[768,128]{1,0:T(8,128)(2,1)S(1)}) custom-call(bf16[128,128]{1,0:T(8,128)(2,1)} %bitcast.21, s32[2,128]{1,0:T(2,128)} %bitcast.22, f32[2,128]{1,0:T(2,128)} %bitcast.23, bf16[512,768]{1,0:T(8,128)(2,1)} %bitcast.16, bf16[512,768]{1,0:T(8,128)(2,1)} %bitcast.17, bf16[128,768]{1,0:T(8,128)(2,1)} %bitcast.18, ...), custom_call_target="tpu_custom_call" | custom-call | tf_op jit(solution)/shard_map/pallas_call | solution.py:335
  50.2 0.6 %copy.12 = bf16[1,128,128]{2,1,0:T(8,128)(2,1)} copy(bf16[1,128,128]{2,1,0:T(8,128)(2,1)S(1)} %bitcast.15) | data formatting | bytes 65536
  50.8 0.7 %copy.13 = bf16[1,1,768,128]{3,2,1,0:T(8,128)(2,1)} copy(bf16[1,1,768,128]{3,2,1,0:T(8,128)(2,1)S(1)} %bitcast.14) | data formatting | bytes 393216

commit v4 on v3

--- a/solution.py
+++ b/solution.py
@@ -33,7 +33,7 @@
 def kernel(
     grad_h, routes_h, prob_h, sg_h, su_h, wg_h, wu_h, wd_h,
     up_out, gd_out,
-    grads, other, meta, routes, prob, sg, su, wg, wu, wd, wd_half, wg_half, wu_half,
+    grads, other, meta, routes, prob, sg, su, wg, wu, wd, wd_half, wide, both,
     pa, ra, sa, r2a, acta,
     fgate, fup, activated, routed, mine, ret, ubuf, vbuf,
     load_sem, x_send, x_recv, m_recv, w_send, w_recv, s1a_send, s1a_recv,
@@ -214,8 +214,10 @@
 
     @pl.when(live)
     def _():
-        to_twin(wg.at[:, twin_half], wg_half, w_send, w_recv.at[1], 0)
-        to_twin(wu.at[:, twin_half], wu_half, w_send, w_recv.at[2], 0)
+        to_twin(wg.at[:, twin_half], wide.at[pl.ds(FEAT, FEAT), pl.ds(0, CA)], w_send, w_recv.at[1], 0)
+        to_twin(wu.at[:, twin_half], wide.at[pl.ds(FEAT, FEAT), pl.ds(CA, CA)], w_send, w_recv.at[2], 0)
+        wide[0:FEAT, 0:CA] = wg[:, my_half]
+        wide[0:FEAT, CA:HID] = wu[:, my_half]
 
     my_y = pl.ds(pl.multiple_of(y * RY, RY), RY)
 
@@ -269,21 +271,28 @@
             await_send(tiles(7), s1a_send)
 
 
-    last = copy(ubuf, vbuf, sec_send, sec_recv, {"section": (s + NS - 1) % NS})
+    lasts = [
+        copy(
+            ubuf.at[pl.ds(at, 32)], vbuf.at[pl.ds(at, 32)], sec_send, sec_recv.at[at // 32],
+            {"section": (s + NS - 1) % NS},
+        )
+        for at in range(0, TOK, 32)
+    ]
 
     @pl.when(live)
     def _():
-        await_recv(wg_half, w_recv.at[1])
-        await_recv(wu_half, w_recv.at[2])
+        await_recv(wide.at[pl.ds(FEAT, FEAT), pl.ds(0, CA)], w_recv.at[1])
+        await_recv(wide.at[pl.ds(FEAT, FEAT), pl.ds(CA, CA)], w_recv.at[2])
         for j in (1, 3, 2, 0):
             await_recv(tiles(7), g2a_recv.at[j])
             value = acta[j].astype(F32)
-            gate = (value * fgate[j]).astype(BF16)
-            up = (value * fup[j]).astype(BF16)
+            both[j, :, 0:CA] = (value * fgate[j]).astype(BF16)
+            both[j, :, CA:HID] = (value * fup[j]).astype(BF16)
+            slot_grads = dot_nt(both[j], wide[...])
             device = {"expert": (x + j) % NX, "dp": twin * NY + y}
-            mine[1, j] = (dot_nt(gate, wg_half[...]) + dot_nt(up, wu_half[...])).astype(BF16)
+            mine[1, j] = slot_grads[:, FEAT:].astype(BF16)
             copy(mine.at[1, j], ret.at[1, j], ret_send, ret_recv.at[1, j], device).start()
-            mine[0, j] = (dot_nt(gate, wg[:, my_half]) + dot_nt(up, wu[:, my_half])).astype(BF16)
+            mine[0, j] = slot_grads[:, :FEAT].astype(BF16)
             if j:
                 device = {"expert": (x + j) % NX}
                 copy(mine.at[0, j], ret.at[0, j], ret_send, ret_recv.at[0, j], device).start()
@@ -293,20 +302,22 @@
             await_recv(ret.at[1, j], ret_recv.at[1, j])
             if j:
                 await_recv(ret.at[0, j], ret_recv.at[0, j])
-        total = grads[0].astype(F32)
-        returned = mine[0, 0].astype(F32) + ret[1, 0].astype(F32)
-        for j in range(1, NX):
-            returned += ret[0, j].astype(F32) + ret[1, j].astype(F32)
-        ubuf[...] = (total + returned).astype(BF16)
-        last.start()
+        for part, last in enumerate(lasts):
+            rows = pl.ds(part * 32, 32)
+            total = grads[0, rows].astype(F32)
+            returned = mine[0, 0, rows].astype(F32) + ret[1, 0, rows].astype(F32)
+            for j in range(1, NX):
+                returned += ret[0, j, rows].astype(F32) + ret[1, j, rows].astype(F32)
+            ubuf[rows, :] = (total + returned).astype(BF16)
+            last.start()
         make_down(256, 256)
         make_down(512, 256)
         for ref, sem in (
-            [(wg_half, w_send), (wu_half, w_send), (grads, ret_send), (grads.at[pl.ds(0, 3)], ret_send)]
+            [(wd_half, w_send), (wd_half, w_send), (grads, ret_send), (grads.at[pl.ds(0, 3)], ret_send)]
             + [(tiles(4), s2a_send)] + [(tiles(7), g2a_send)] * NX
         ):
             await_send(ref, sem)
-        last.wait_send()
+        await_send(ubuf, sec_send)
 
     @pl.when(s == 0)
     def _():
@@ -325,7 +336,8 @@
 
     @pl.when(s != NS - 1)
     def _():
-        last.wait_recv()
+        for last in lasts:
+            last.wait_recv()
         up_out[...] = vbuf[...]
 
 
@@ -352,8 +364,8 @@
             vmem((FEAT, HID), BF16),
             vmem((HID, FEAT), BF16),
             vmem((CA, FEAT), BF16),
-            vmem((FEAT, CA), BF16),
-            vmem((FEAT, CA), BF16),
+            vmem((2 * FEAT, HID), BF16),
+            vmem((NX, TOK, HID), BF16),
             vmem((NX, TOK, CA), BF16),
             vmem((NX, NY - 1, RY, CA), BF16),
             vmem((NX, RY, CA), BF16),
@@ -371,7 +383,7 @@
             dma, dma((2, NX)), dma((NX,)),
             dma, dma((3,)), dma, dma((NX,)),
             dma, dma((NX,)), dma, dma((NX,)),
-            dma, dma((2, NX)), dma, dma,
+            dma, dma((2, NX)), dma, dma((4,)),
             pltpu.SemaphoreType.REGULAR,
         ],
         compiler_params=pltpu.CompilerParams(

time: 51.7 us -> 51.6 us (level)
  no operation moved by 1% of the time
where the time goes in v4:
time: 51.6 us; the launch traced here: 51.4 us
  Pallas kernels  49.5 us (96%)
  local copies, waits for them, and re-layouts  1.29 us (2%)
  between operations  0.64 us (1%)
    pallas_call x1, Pallas kernels, on_device(): pl.pallas_call(kernel, out_shape=(jax.ShapeDtypeStruct((TOK, FEAT), BF16)...  49.5 us
    unnamed x2, local copies, waits for them, and re-layouts  1.29 us

profile of v4, /device:TPU:1, one launch (start us, length us, event | category | flops | bytes accessed | tf_op | source)
XLA Modules:
  0.0 51.4 jit_solution(10976416921711350879)
XLA Ops:
  0.6 49.5 %shard_map.95 = (bf16[128,128]{1,0:T(8,128)(2,1)S(1)}, bf16[768,128]{1,0:T(8,128)(2,1)S(1)}) custom-call(bf16[128,128]{1,0:T(8,128)(2,1)} %bitcast.21, s32[2,128]{1,0:T(2,128)} %bitcast.22, f32[2,128]{1,0:T(2,128)} %bitcast.23, bf16[512,768]{1,0:T(8,128)(2,1)} %bitcast.16, bf16[512,768]{1,0:T(8,128)(2,1)} %bitcast.17, bf16[128,768]{1,0:T(8,128)(2,1)} %bitcast.18, ...), custom_call_target="tpu_custom_call" | custom-call | tf_op jit(solution)/shard_map/pallas_call | solution.py:347
  50.1 0.6 %copy.12 = bf16[1,128,128]{2,1,0:T(8,128)(2,1)} copy(bf16[1,128,128]{2,1,0:T(8,128)(2,1)S(1)} %bitcast.15) | data formatting | bytes 65536
  50.7 0.7 %copy.13 = bf16[1,1,768,128]{3,2,1,0:T(8,128)(2,1)} copy(bf16[1,1,768,128]{3,2,1,0:T(8,128)(2,1)S(1)} %bitcast.14) | data formatting | bytes 393216

commit v5 on v4

--- a/solution.py
+++ b/solution.py
@@ -82,7 +82,7 @@
         loads[name].start()
 
     barrier = pltpu.get_barrier_semaphore()
-    greet = [dp(z, at_y(k)) for k in range(1, NY)] + [dp(far, y)]
+    greet = [dp(z, at_y(k)) for k in Y_ORDER] + [dp(far, y)]
     greet += [{"expert": (x + k) % NX} for k in range(1, NX)]
     greet += [{"expert": (x + k) % NX, "dp": twin * NY + y} for k in range(NX)]
     for device in greet:
@@ -254,10 +254,10 @@
     def _():
         second(0)
         second(1)
+        pass_turn()
+        reduce_rest()
         for j in range(NX):
             await_send(tiles(7), s1a_send)
-        pass_turn()
-        reduce_rest()
 
     @pl.when(second_half)
     def _():

time: 51.6 us -> 51.6 us (level)
  no operation moved by 1% of the time
where the time goes in v5:
time: 51.6 us; the launch traced here: 51.4 us
  Pallas kernels  49.5 us (96%)
  local copies, waits for them, and re-layouts  1.29 us (2%)
  between operations  0.64 us (1%)
    pallas_call x1, Pallas kernels, on_device(): pl.pallas_call(kernel, out_shape=(jax.ShapeDtypeStruct((TOK, FEAT), BF16)...  49.5 us
    unnamed x2, local copies, waits for them, and re-layouts  1.29 us

profile of v5, /device:TPU:1, one launch (start us, length us, event | category | flops | bytes accessed | tf_op | source)
XLA Modules:
  0.0 51.4 jit_solution(12232359751756583941)
XLA Ops:
  0.6 49.5 %shard_map.95 = (bf16[128,128]{1,0:T(8,128)(2,1)S(1)}, bf16[768,128]{1,0:T(8,128)(2,1)S(1)}) custom-call(bf16[128,128]{1,0:T(8,128)(2,1)} %bitcast.21, s32[2,128]{1,0:T(2,128)} %bitcast.22, f32[2,128]{1,0:T(2,128)} %bitcast.23, bf16[512,768]{1,0:T(8,128)(2,1)} %bitcast.16, bf16[512,768]{1,0:T(8,128)(2,1)} %bitcast.17, bf16[128,768]{1,0:T(8,128)(2,1)} %bitcast.18, ...), custom_call_target="tpu_custom_call" | custom-call | tf_op jit(solution)/shard_map/pallas_call | solution.py:347
  50.1 0.6 %copy.12 = bf16[1,128,128]{2,1,0:T(8,128)(2,1)} copy(bf16[1,128,128]{2,1,0:T(8,128)(2,1)S(1)} %bitcast.15) | data formatting | bytes 65536
  50.8 0.7 %copy.13 = bf16[1,1,768,128]{3,2,1,0:T(8,128)(2,1)} copy(bf16[1,1,768,128]{3,2,1,0:T(8,128)(2,1)S(1)} %bitcast.14) | data formatting | bytes 393216
